TPU v7x, 32 devices: a whole 2x2x4 slice. The times are simulated.
32 devices in a mesh: dp: 4 (over y, core), fsdp: 8 (over z, x).
Axes of the slice: x: 2, y: 2, z: 4, core: 2. Of those that a mesh axis runs over, the one named last changes fastest.
Arguments:
- frames: bfloat16 [16384, 768], P(('dp', 'fsdp')), may hold values from -6 to 6
- lengths: int32 [32, 2], P(('dp', 'fsdp')), may hold values from 0 to 512, as said below
- query_weight: bfloat16 [768, 768], P(('dp', 'fsdp')), may hold values from -0.21875 to 0.21875
- query_bias: bfloat16 [768], P(('dp', 'fsdp')), may hold values from -3 to 3
- key_weight: bfloat16 [768, 768], P(('dp', 'fsdp')), may hold values from -0.21875 to 0.21875
- value_weight: bfloat16 [768, 768], P(('dp', 'fsdp')), may hold values from -0.21875 to 0.21875
- value_bias: bfloat16 [768], P(('dp', 'fsdp')), may hold values from -3 to 3
- output_weight: bfloat16 [768, 768], P(('dp', 'fsdp')), may hold values from -2.5 to 2.5
- output_bias: bfloat16 [768], P(('dp', 'fsdp')), may hold values from -3 to 3
- first_gain: bfloat16 [768], P(('dp', 'fsdp')), may hold values from 0.5 to 1.5
- first_shift: bfloat16 [768], P(('dp', 'fsdp')), may hold values from -3 to 3
- inner_weight: bfloat16 [768, 3072], P(('dp', 'fsdp')), may hold values from -0.21875 to 0.21875
- inner_bias: bfloat16 [3072], P(('dp', 'fsdp')), may hold values from -3 to 3
- outer_weight: bfloat16 [3072, 768], P(('dp', 'fsdp')), may hold values from -0.109375 to 0.109375
- outer_bias: bfloat16 [768], P(('dp', 'fsdp')), may hold values from -3 to 3
- second_gain: bfloat16 [768], P(('dp', 'fsdp')), may hold values from 0.5 to 1.5
- second_shift: bfloat16 [768], P(('dp', 'fsdp')), may hold values from -3 to 3
- grad_out: bfloat16 [16384, 768], P(('dp', 'fsdp')), may hold values from -6 to 6
Outputs:
- layer_out: bfloat16 [16384, 768], P(('dp', 'fsdp'))
- frames_grad: bfloat16 [16384, 768], P(('dp', 'fsdp'))
- query_weight_grad: float32 [768, 768], P(('dp', 'fsdp'))
- query_bias_grad: float32 [768], P(('dp', 'fsdp'))
- key_weight_grad: float32 [768, 768], P(('dp', 'fsdp'))
- value_weight_grad: float32 [768, 768], P(('dp', 'fsdp'))
- value_bias_grad: float32 [768], P(('dp', 'fsdp'))
- output_weight_grad: float32 [768, 768], P(('dp', 'fsdp'))
- output_bias_grad: float32 [768], P(('dp', 'fsdp'))
- first_gain_grad: float32 [768], P(('dp', 'fsdp'))
- first_shift_grad: float32 [768], P(('dp', 'fsdp'))
- inner_weight_grad: float32 [768, 3072], P(('dp', 'fsdp'))
- inner_bias_grad: float32 [3072], P(('dp', 'fsdp'))
- outer_weight_grad: float32 [3072, 768], P(('dp', 'fsdp'))
- outer_bias_grad: float32 [768], P(('dp', 'fsdp'))
- second_gain_grad: float32 [768], P(('dp', 'fsdp'))
- second_shift_grad: float32 [768], P(('dp', 'fsdp'))
Inputs may be any that keep to these rules, and one draw needn't show every extreme that they name: `lengths`: row b holds block b's two utterances: slot 0 has 100 to 512 frames, slot 1 has 0 (empty) up to 512 minus slot 0; the block's remaining slots are padding. In one block, drawn from the seed, slot 0 fills all 512 slots.
All inputs are finite; a program needn't handle non-finite values.
Results may differ from a plain program's by a relative error of at most 0.015.
Values may be sent and summed in bfloat16 or wider, within the bound.
A program may use at most 192 MiB of HBM per device.

v0:
```python
import jax
import jax.numpy as jnp
from jax import lax
from jax.sharding import PartitionSpec as P

HEADS = 12


def layer_norm(values, gain_vec, shift_vec):
    center = values - jnp.mean(values, axis=-1, keepdims=True)
    spread = jnp.mean(center * center, axis=-1, keepdims=True)
    return center * lax.rsqrt(spread + 1e-05) * gain_vec + shift_vec


def exact_gelu(values):
    return jax.nn.gelu(values, approximate=False)


def matmul(left_side, right_side):
    return jnp.dot(left_side, right_side, preferred_element_type=jnp.float32)


def matmul_tn(left_side, right_side):
    return lax.dot_general(
        left_side, right_side, (((0,), (0,)), ((), ())), preferred_element_type=jnp.float32
    )


def matmul_nt(left_side, right_side):
    return lax.dot_general(
        left_side, right_side, (((1,), (1,)), ((), ())), preferred_element_type=jnp.float32
    )


def column_sums(values):
    return jnp.sum(values.astype(jnp.float32), axis=0)


def block_scores(query_block, key_heads, group_block, groups, score_scale):
    raw_scores = (
        jnp.einsum("qhd,khd->hqk", query_block, key_heads, preferred_element_type=jnp.float32)
        * score_scale
    )
    allowed = group_block[:, None] == groups[None, :]
    return jnp.where(allowed[None], raw_scores, -1e30)


def per_device(
    frames,
    lengths,
    query_weight,
    query_bias,
    key_weight,
    value_weight,
    value_bias,
    output_weight,
    output_bias,
    first_gain,
    first_shift,
    inner_weight,
    inner_bias,
    outer_weight,
    outer_bias,
    second_gain,
    second_shift,
    grad_out,
):
    frame_count = frames.shape[0]
    model_width = frames.shape[1]
    head_size = model_width // HEADS
    score_scale = head_size ** (-0.5)
    places = jnp.arange(frame_count, dtype=jnp.int32)
    bounds = jnp.cumsum(lengths[0])
    groups = jnp.sum((places[:, None] >= bounds[None, :]).astype(jnp.int32), axis=1)
    live_mask = (places < bounds[-1]).astype(jnp.float32)
    gathered = (
        lax.all_gather(query_weight, ("dp", "fsdp"), axis=0, tiled=True),
        lax.all_gather(query_bias, ("dp", "fsdp"), axis=0, tiled=True),
        lax.all_gather(key_weight, ("dp", "fsdp"), axis=0, tiled=True),
        lax.all_gather(value_weight, ("dp", "fsdp"), axis=0, tiled=True),
        lax.all_gather(value_bias, ("dp", "fsdp"), axis=0, tiled=True),
        lax.all_gather(output_weight, ("dp", "fsdp"), axis=0, tiled=True),
        lax.all_gather(output_bias, ("dp", "fsdp"), axis=0, tiled=True),
        lax.all_gather(first_gain, ("dp", "fsdp"), axis=0, tiled=True),
        lax.all_gather(first_shift, ("dp", "fsdp"), axis=0, tiled=True),
        lax.all_gather(inner_weight, ("dp", "fsdp"), axis=0, tiled=True),
        lax.all_gather(inner_bias, ("dp", "fsdp"), axis=0, tiled=True),
        lax.all_gather(outer_weight, ("dp", "fsdp"), axis=0, tiled=True),
        lax.all_gather(outer_bias, ("dp", "fsdp"), axis=0, tiled=True),
        lax.all_gather(second_gain, ("dp", "fsdp"), axis=0, tiled=True),
        lax.all_gather(second_shift, ("dp", "fsdp"), axis=0, tiled=True),
    )
    (
        query_mat,
        query_vec,
        key_mat,
        value_mat,
        value_vec,
        output_mat,
        output_vec,
        first_scale,
        first_offset,
        inner_mat,
        inner_vec,
        outer_mat,
        outer_vec,
        second_scale,
        second_offset,
    ) = gathered
    query_rows = (matmul(frames, query_mat) + query_vec.astype(jnp.float32)).astype(jnp.bfloat16)
    key_rows = matmul(frames, key_mat).astype(jnp.bfloat16)
    value_rows = (matmul(frames, value_mat) + value_vec.astype(jnp.float32)).astype(jnp.bfloat16)
    query_heads = query_rows.reshape(frame_count, HEADS, head_size)
    key_heads = key_rows.reshape(frame_count, HEADS, head_size)
    value_heads = value_rows.reshape(frame_count, HEADS, head_size)
    scores = block_scores(query_heads, key_heads, groups, groups, score_scale)
    row_max = jnp.max(scores, axis=-1, keepdims=True)
    raw_weights = jnp.exp(scores - row_max)
    row_total = jnp.sum(raw_weights, axis=-1, keepdims=True)
    attn_prob = raw_weights / row_total
    log_totals = row_max + jnp.log(row_total)
    context_parts = jnp.einsum(
        "hqk,khd->qhd",
        attn_prob.astype(jnp.bfloat16),
        value_heads,
        preferred_element_type=jnp.float32,
    )
    context_rows = context_parts.reshape(frame_count, model_width).astype(jnp.bfloat16)
    frames_float = frames.astype(jnp.float32)
    resid_one = frames_float + matmul(context_rows, output_mat) + output_vec.astype(jnp.float32)
    hidden, first_pull = jax.vjp(
        layer_norm, resid_one, first_scale.astype(jnp.float32), first_offset.astype(jnp.float32)
    )
    hidden_low = hidden.astype(jnp.bfloat16)
    inner_pre = matmul(hidden_low, inner_mat) + inner_vec.astype(jnp.float32)
    active, gelu_pull = jax.vjp(exact_gelu, inner_pre)
    active_low = active.astype(jnp.bfloat16)
    outer_out = matmul(active_low, outer_mat) + outer_vec.astype(jnp.float32)
    normed_out, second_pull = jax.vjp(
        layer_norm,
        hidden + outer_out,
        second_scale.astype(jnp.float32),
        second_offset.astype(jnp.float32),
    )
    layer_out = (normed_out * live_mask[:, None]).astype(jnp.bfloat16)
    regathered = (
        lax.all_gather(query_weight, ("dp", "fsdp"), axis=0, tiled=True),
        lax.all_gather(key_weight, ("dp", "fsdp"), axis=0, tiled=True),
        lax.all_gather(value_weight, ("dp", "fsdp"), axis=0, tiled=True),
        lax.all_gather(output_weight, ("dp", "fsdp"), axis=0, tiled=True),
        lax.all_gather(inner_weight, ("dp", "fsdp"), axis=0, tiled=True),
        lax.all_gather(outer_weight, ("dp", "fsdp"), axis=0, tiled=True),
    )
    query_mat, key_mat, value_mat, output_mat, inner_mat, outer_mat = regathered
    grad_top = grad_out.astype(jnp.float32) * live_mask[:, None]
    grad_two, second_gain_grad, second_shift_grad = second_pull(grad_top)
    grad_outer = grad_two.astype(jnp.bfloat16)
    outer_mat_grad = matmul_tn(active_low, grad_outer)
    outer_vec_grad = column_sums(grad_outer)
    (grad_inner,) = gelu_pull(matmul_nt(grad_outer, outer_mat))
    grad_inner_low = grad_inner.astype(jnp.bfloat16)
    inner_mat_grad = matmul_tn(hidden_low, grad_inner_low)
    inner_vec_grad = column_sums(grad_inner_low)
    grad_hidden = grad_two + matmul_nt(grad_inner_low, inner_mat)
    grad_one, first_gain_grad, first_shift_grad = first_pull(grad_hidden)
    grad_attn = grad_one.astype(jnp.bfloat16)
    output_mat_grad = matmul_tn(context_rows, grad_attn)
    output_vec_grad = column_sums(grad_attn)
    grad_context = (
        matmul_nt(grad_attn, output_mat).astype(jnp.bfloat16).reshape(frame_count, HEADS, head_size)
    )
    scores = block_scores(query_heads, key_heads, groups, groups, score_scale)
    attn_prob = jnp.exp(scores - log_totals)
    grad_prob = jnp.einsum(
        "qhd,khd->hqk", grad_context, value_heads, preferred_element_type=jnp.float32
    )
    inner_sum = jnp.sum(attn_prob * grad_prob, axis=-1, keepdims=True)
    grad_scores = (attn_prob * (grad_prob - inner_sum)).astype(jnp.bfloat16)
    query_grad_parts = (
        jnp.einsum("hqk,khd->qhd", grad_scores, key_heads, preferred_element_type=jnp.float32)
        * score_scale
    )
    key_grad_sum = (
        jnp.einsum("hqk,qhd->khd", grad_scores, query_heads, preferred_element_type=jnp.float32)
        * score_scale
    )
    value_grad_sum = jnp.einsum(
        "hqk,qhd->khd",
        attn_prob.astype(jnp.bfloat16),
        grad_context,
        preferred_element_type=jnp.float32,
    )
    grad_query = query_grad_parts.reshape(frame_count, model_width).astype(jnp.bfloat16)
    grad_key = key_grad_sum.reshape(frame_count, model_width).astype(jnp.bfloat16)
    grad_value = value_grad_sum.reshape(frame_count, model_width).astype(jnp.bfloat16)
    query_mat_grad = matmul_tn(frames, grad_query)
    query_vec_grad = column_sums(grad_query)
    key_mat_grad = matmul_tn(frames, grad_key)
    value_mat_grad = matmul_tn(frames, grad_value)
    value_vec_grad = column_sums(grad_value)
    frames_grad = (
        grad_one
        + matmul_nt(grad_query, query_mat)
        + matmul_nt(grad_key, key_mat)
        + matmul_nt(grad_value, value_mat)
    ).astype(jnp.bfloat16)
    shares = (
        lax.psum_scatter(query_mat_grad, ("dp", "fsdp"), scatter_dimension=0, tiled=True),
        lax.psum_scatter(query_vec_grad, ("dp", "fsdp"), scatter_dimension=0, tiled=True),
        lax.psum_scatter(key_mat_grad, ("dp", "fsdp"), scatter_dimension=0, tiled=True),
        lax.psum_scatter(value_mat_grad, ("dp", "fsdp"), scatter_dimension=0, tiled=True),
        lax.psum_scatter(value_vec_grad, ("dp", "fsdp"), scatter_dimension=0, tiled=True),
        lax.psum_scatter(output_mat_grad, ("dp", "fsdp"), scatter_dimension=0, tiled=True),
        lax.psum_scatter(output_vec_grad, ("dp", "fsdp"), scatter_dimension=0, tiled=True),
        lax.psum_scatter(first_gain_grad, ("dp", "fsdp"), scatter_dimension=0, tiled=True),
        lax.psum_scatter(first_shift_grad, ("dp", "fsdp"), scatter_dimension=0, tiled=True),
        lax.psum_scatter(inner_mat_grad, ("dp", "fsdp"), scatter_dimension=0, tiled=True),
        lax.psum_scatter(inner_vec_grad, ("dp", "fsdp"), scatter_dimension=0, tiled=True),
        lax.psum_scatter(outer_mat_grad, ("dp", "fsdp"), scatter_dimension=0, tiled=True),
        lax.psum_scatter(outer_vec_grad, ("dp", "fsdp"), scatter_dimension=0, tiled=True),
        lax.psum_scatter(second_gain_grad, ("dp", "fsdp"), scatter_dimension=0, tiled=True),
        lax.psum_scatter(second_shift_grad, ("dp", "fsdp"), scatter_dimension=0, tiled=True),
    )
    return (
        layer_out,
        frames_grad,
        shares[0],
        shares[1],
        shares[2],
        shares[3],
        shares[4],
        shares[5],
        shares[6],
        shares[7],
        shares[8],
        shares[9],
        shares[10],
        shares[11],
        shares[12],
        shares[13],
        shares[14],
    )


def solution(mesh):
    in_specs = (
        P(("dp", "fsdp"), None),
        P(("dp", "fsdp"), None),
        P(("dp", "fsdp"), None),
        P(("dp", "fsdp")),
        P(("dp", "fsdp"), None),
        P(("dp", "fsdp"), None),
        P(("dp", "fsdp")),
        P(("dp", "fsdp"), None),
        P(("dp", "fsdp")),
        P(("dp", "fsdp")),
        P(("dp", "fsdp")),
        P(("dp", "fsdp"), None),
        P(("dp", "fsdp")),
        P(("dp", "fsdp"), None),
        P(("dp", "fsdp")),
        P(("dp", "fsdp")),
        P(("dp", "fsdp")),
        P(("dp", "fsdp"), None),
    )
    out_specs = (
        P(("dp", "fsdp"), None),
        P(("dp", "fsdp"), None),
        P(("dp", "fsdp"), None),
        P(("dp", "fsdp")),
        P(("dp", "fsdp"), None),
        P(("dp", "fsdp"), None),
        P(("dp", "fsdp")),
        P(("dp", "fsdp"), None),
        P(("dp", "fsdp")),
        P(("dp", "fsdp")),
        P(("dp", "fsdp")),
        P(("dp", "fsdp"), None),
        P(("dp", "fsdp")),
        P(("dp", "fsdp"), None),
        P(("dp", "fsdp")),
        P(("dp", "fsdp")),
        P(("dp", "fsdp")),
    )
    return jax.shard_map(
        per_device, mesh=mesh, in_specs=in_specs, out_specs=out_specs, check_vma=False
    )
```

profile of v0, /device:TPU:24, one launch (start us, length us, event | category | flops | bytes accessed | tf_op | source)
XLA Modules:
  0.0 1123.3 jit_solution(8192119810610155402)
XLA Ops:
  11.2 0.8 dynamic-update-slice
  12.1 0.8 dynamic-update-slice.1
  12.9 0.8 dynamic-update-slice.2
  13.7 0.8 dynamic-update-slice.4
  14.6 0.8 dynamic-update-slice.3
  15.4 0.8 dynamic-update-slice.6
  16.2 0.8 dynamic-update-slice.8
  17.1 0.8 dynamic-update-slice.7
  17.9 0.8 dynamic-update-slice.5
  18.8 39.7 %all-reduce.19 = (bf16[768]{0:T(1024)(128)(2,1)S(1)}, bf16[768]{0:T(1024)(128)(2,1)S(1)}, bf16[768]{0:T(1024)(128)(2,1)S(1)}, bf16[768]{0:T(1024)(128)(2,1)S(1)}...) all-reduce(bf16[768]{0:T(1024)(128)(2,1)S(1)} %dynamic-update-slice, ...), channel_id=1, replica_groups=mesh['dp'=4,'fsdp'=8] {'dp','fsdp'}, use_global_device_ids=true, to_apply=%add | all-reduce | flops 9216 | bytes 36864
  58.5 0.8 reduce-window.4
  60.9 4.3 all-gather.7.cloned.1.call-done
  65.3 2.3 add_convert_fusion.3
  67.6 54.0 %all-gather.9.cloned.1.call-done = bf16[768,768]{1,0:T(8,128)(2,1)} async-done(((bf16[24,768]{1,0:T(8,128)(2,1)}), bf16[768,768]{1,0:T(8,128)(2,1)}) %all-gather.9.cloned.1.call-update) | async-done | bytes 1179664 | tf_op jit(solution)/shard_map/all_gather | solution.py:77
  121.6 2.9 add_convert_fusion.2
  124.8 1.7 copy.73
  126.5 51.2 %all-gather.11.cloned.1.call-done = bf16[768,768]{1,0:T(8,128)(2,1)} async-done(((bf16[24,768]{1,0:T(8,128)(2,1)}), bf16[768,768]{1,0:T(8,128)(2,1)}) %all-gather.11.cloned.1.call-update) | async-done | bytes 1179664 | tf_op jit(solution)/shard_map/all_gather | solution.py:79
  177.7 2.9 convolution_convert_fusion.1
  180.6 1.4 copy.74
  182.0 2.1 fusion.12
  184.1 2.6 fusion
  186.7 2.0 copy-done
  188.7 4.4 fusion.18
  193.0 40.6 %all-gather.13.cloned.1.call-done = bf16[768,768]{1,0:T(8,128)(2,1)} async-done(((bf16[24,768]{1,0:T(8,128)(2,1)}), bf16[768,768]{1,0:T(8,128)(2,1)}) %all-gather.13.cloned.1.call-update) | async-done | bytes 1179664 | tf_op jit(solution)/shard_map/all_gather | solution.py:82
  233.7 2.4 fusion.35
  236.1 1.1 copy-done.7
  237.6 61.4 %all-gather.15.cloned.1.call-done = bf16[768,3072]{1,0:T(8,128)(2,1)} async-done(((bf16[24,3072]{1,0:T(8,128)(2,1)}), bf16[768,3072]{1,0:T(8,128)(2,1)}) %all-gather.15.cloned.1.call-update) | async-done | bytes 4718608 | tf_op jit(solution)/shard_map/all_gather | solution.py:86
  299.0 21.0 %multiply_convert_fusion.1 = (bf16[512,3072]{1,0:T(8,128)(2,1)}, f32[512,3072]{1,0:T(8,128)}, f32[512,3072]{1,0:T(8,128)}) fusion(f32[3072]{0:T(1024)S(1)} %convert_element_type.159, bf16[768,3072]{1,0:T(8,128)(2,1)} %all-gather.15.cloned.1.call-done, f32[512,768]{1,0:T(8,128)} %copy-done.7, f32[768]{0:T(1024)S(1)} %convert_element_type.157, ...), kind=kOutput, calls=%fused_computation.14 | convolution fusion | flops 2521694208 | bytes 22042624 | tf_op jit(solution)/shard_map/dot_general | solution.py:20
  320.0 44.4 %all-gather.17.cloned.1.call-done = bf16[3072,768]{1,0:T(8,128)(2,1)} async-done(((bf16[96,768]{1,0:T(8,128)(2,1)}), bf16[3072,768]{1,0:T(8,128)(2,1)}) %all-gather.17.cloned.1.call-update) | async-done | bytes 4718608 | tf_op jit(solution)/shard_map/all_gather | solution.py:88
  364.4 6.1 fusion.36
  371.7 1.7 fusion.33
  374.3 8.7 convert_reduce_fusion
  383.0 3.1 multiply_reduce_fusion.2
  387.1 0.9 copy-done.14
  387.9 1.7 convolution_convert_fusion
  389.6 2.3 copy.76
  392.0 13.5 %multiply_reduce_fusion = (f32[12,512]{1,0:T(8,128)S(1)}, f32[12,512,512]{1,2,0:T(8,128)}) fusion(f32[12,512]{1,0:T(8,128)S(1)} %log_add_fusion, f32[12,512,512]{1,2,0:T(8,128)} %copy-done, pred[512,512]{0,1:T(8,128)(4,1)S(1)} %broadcast_compare_fusion, bf16[512,12,64]{0,2,1:T(8,128)(2,1)} %bitcast.82, bf16[512,12,64]{0,2,1:T(8,128)(2,1)} %bitcast.81), kind=kOutput, calls=%fused_computation.1 | convolution fusion | flops 418375680 | bytes 27049984 | tf_op jit(solution)/shard_map/qhd,khd->hqk/dot_general | solution.py:174
  405.5 7.0 multiply_convert_fusion
  412.5 1.2 convert_reduce_fusion.4
  413.7 1.4 copy-done.1
  415.1 0.9 copy-done.5
  416.0 2.2 convolution_bitcast_fusion.2
  418.2 3.1 copy.87
  421.6 4.8 multiply_convert_fusion.2
  426.4 0.9 copy-done.17
  427.3 2.2 convolution_bitcast_fusion.1
  429.5 3.2 copy.89
  432.8 6.6 convert_reduce_fusion.3
  439.4 0.9 copy-done.15
  440.3 2.2 convolution_bitcast_fusion
  442.5 3.2 copy.91
  445.8 3.7 fusion.39
  449.6 7.3 fusion.28
  456.9 1.1 copy-done.21
  458.0 8.2 fusion.40
  466.4 40.3 %all-reduce.18 = (f32[768]{0:T(1024)S(1)}, f32[768]{0:T(1024)S(1)}, f32[768]{0:T(1024)S(1)}, f32[768]{0:T(1024)S(1)}, f32[768]{0:T(1024)S(1)}, /*index=5*/f32[30...) all-reduce(f32[768]{0:T(1024)S(1)} %reduce_sum.228, ...), channel_id=3, replica_groups=mesh['dp'=4,'fsdp'=8] {'dp','fsdp'}, use_global_device_ids=true, to_apply=%region_15.16.clone | all-reduce | flops 9216 | bytes 73728
  511.9 2.2 fusion.38
  515.1 2.0 add_convert_fusion.1
  517.0 2.9 reduce-scatter.19.cloned.1.call-done
  519.9 104.7 %reduce-scatter.21.cloned.1.call-done = f32[24,768]{1,0:T(8,128)} async-done(((f32[768,768]{1,0:T(8,128)}), f32[24,768]{1,0:T(8,128)}) %reduce-scatter.21.cloned.1.call-update) | async-done | bytes 73744
  624.7 104.0 %reduce-scatter.23.cloned.1.call-done = f32[24,768]{1,0:T(8,128)} async-done(((f32[768,768]{1,0:T(8,128)}), f32[24,768]{1,0:T(8,128)}) %reduce-scatter.23.cloned.1.call-update) | async-done | bytes 73744
  728.6 104.6 %reduce-scatter.13.cloned.1.call-done = f32[24,768]{1,0:T(8,128)} async-done(((f32[768,768]{1,0:T(8,128)}), f32[24,768]{1,0:T(8,128)}) %reduce-scatter.13.cloned.1.call-update) | async-done | bytes 73744 | tf_op jit(solution)/shard_map/reduce_scatter | solution.py:213
  833.2 141.0 %reduce-scatter.15.cloned.1.call-done = f32[24,3072]{1,0:T(8,128)} async-done(((f32[768,3072]{1,0:T(8,128)}), f32[24,3072]{1,0:T(8,128)}) %reduce-scatter.15.cloned.1.call-update) | async-done | bytes 294928 | tf_op jit(solution)/shard_map/reduce_scatter | solution.py:217
  974.2 141.9 %reduce-scatter.17.cloned.1.call-done = f32[96,768]{1,0:T(8,128)} async-done(((f32[3072,768]{1,0:T(8,128)}), f32[96,768]{1,0:T(8,128)}) %reduce-scatter.17.cloned.1.call-update) | async-done | bytes 294928 | tf_op jit(solution)/shard_map/reduce_scatter | solution.py:219
  (130 shorter events, 15.8 us)
Async XLA Ops:
  7.2 114.4 %copy-start.2 = (bf16[512,768]{1,0:T(8,128)(2,1)S(1)}, bf16[512,768]{1,0:T(8,128)(2,1)}, u32[]{:S(2)}) copy-start(bf16[512,768]{1,0:T(8,128)(2,1)} %param.18) | copy-start | bytes 2359300
  7.2 58.1 %all-gather.7.cloned.1.call-start = ((), (), s32[]{:S(2)}) async-start(), calls=%async_computation.6 | async-start | bytes 1216512 | tf_op jit(solution)/shard_map/all_gather | solution.py:80
  7.9 113.7 %all-gather.9.cloned.1.call-start = ((), (), s32[]{:S(2)}) async-start(), calls=%async_computation.7 | async-start | bytes 1216512 | tf_op jit(solution)/shard_map/all_gather | solution.py:77
  8.7 169.0 %all-gather.11.cloned.1.call-start = ((), (), s32[]{:S(2)}) async-start(), calls=%async_computation.8 | async-start | bytes 1216512 | tf_op jit(solution)/shard_map/all_gather | solution.py:79
  9.4 224.3 %all-gather.13.cloned.1.call-start = ((), (), s32[]{:S(2)}) async-start(), calls=%async_computation.9 | async-start | bytes 1216512 | tf_op jit(solution)/shard_map/all_gather | solution.py:82
  10.0 289.0 %all-gather.15.cloned.1.call-start = ((), (), s32[]{:S(2)}) async-start(), calls=%async_computation.10 | async-start | bytes 4866048 | tf_op jit(solution)/shard_map/all_gather | solution.py:86
  10.6 353.8 %all-gather.17.cloned.1.call-start = ((), (), s32[]{:S(2)}) async-start(), calls=%async_computation.11 | async-start | bytes 4866048 | tf_op jit(solution)/shard_map/all_gather | solution.py:88
  11.2 508.8 %reduce-scatter.19.cloned.1.call-start = ((), (), s32[]{:S(2)}) async-start(), calls=%async_computation.15 | async-start | bytes 2433024
  124.8 61.9 %copy-start.11 = (bf16[512,768]{0,1:T(8,128)(2,1)}, bf16[512,768]{0,1:T(8,128)(2,1)S(1)}, u32[]{:S(2)}) copy-start(bf16[512,768]{0,1:T(8,128)(2,1)S(1)} %copy.72) | copy-start | bytes 2359300
  184.1 4.6 copy-start
  236.1 1.1 copy-start.7
  237.6 126.8 %copy-start.8 = (f32[512,768]{1,0:T(8,128)S(1)}, f32[512,768]{1,0:T(8,128)}, u32[]{:S(2)}) copy-start(f32[512,768]{1,0:T(8,128)} %copy-done.7) | copy-start | bytes 4718596
  364.4 6.4 copy-start.13
  371.6 2.6 copy-start.22
  373.4 9.6 slice-start.3
  373.6 9.3 copy-start.20
  374.3 8.7 slice-start.4
  382.9 3.2 copy-start.25
  383.0 3.2 copy-start.9
  386.2 1.8 copy-start.24
  387.0 0.9 copy-start.14
  392.0 13.5 %slice-start = ((s8[12582912]{0:T(1024)(128)(4,1)}), s8[4194304]{0:T(1024)(128)(4,1)S(1)}, s32[]{:S(2)}) async-start(s8[12582912]{0:T(1024)(128)(4,1)} %bitcast.72), calls=%async_computation.18 | async-start | bytes 8388608
  392.0 13.5 %slice-start.1 = ((s8[12582912]{0:T(1024)(128)(4,1)}), s8[4194304]{0:T(1024)(128)(4,1)S(1)}, s32[]{:S(2)}) async-start(s8[12582912]{0:T(1024)(128)(4,1)} %bitcast.72), calls=%async_computation.19 | async-start | bytes 8388608
  392.0 13.5 %slice-start.2 = ((s8[12582912]{0:T(1024)(128)(4,1)}), s8[4194304]{0:T(1024)(128)(4,1)S(1)}, s32[]{:S(2)}) async-start(s8[12582912]{0:T(1024)(128)(4,1)} %bitcast.72), calls=%async_computation.20 | async-start | bytes 8388608
  412.5 2.6 copy-start.1
  412.5 3.5 copy-start.3
  415.1 0.9 copy-start.5
  421.3 6.0 copy-start.4
  421.3 203.3 %reduce-scatter.21.cloned.1.call-start = ((), (), s32[]{:S(2)}) async-start(), calls=%async_computation.16 | async-start | bytes 2433024
  426.4 0.9 copy-start.17
  429.5 3.3 copy-start.12
  432.7 295.9 %reduce-scatter.23.cloned.1.call-start = ((), (), s32[]{:S(2)}) async-start(), calls=%async_computation.17 | async-start | bytes 2433024
  439.4 0.9 copy-start.15
  445.7 3.8 copy-start.10
  445.7 387.5 %reduce-scatter.13.cloned.1.call-start = ((), (), s32[]{:S(2)}) async-start(), calls=%async_computation.12 | async-start | bytes 2433024 | tf_op jit(solution)/shard_map/reduce_scatter | solution.py:213
  449.5 524.7 %reduce-scatter.15.cloned.1.call-start = ((), (), s32[]{:S(2)}) async-start(), calls=%async_computation.13 | async-start | bytes 9732096 | tf_op jit(solution)/shard_map/reduce_scatter | solution.py:217
  456.8 1.1 copy-start.21
  456.8 659.3 %reduce-scatter.17.cloned.1.call-start = ((), (), s32[]{:S(2)}) async-start(), calls=%async_computation.14 | async-start | bytes 9732096 | tf_op jit(solution)/shard_map/reduce_scatter | solution.py:219
  466.2 45.7 %copy-start.18 = (bf16[12,64,512]{2,1,0:T(8,128)(2,1)S(1)}, bf16[12,64,512]{2,1,0:T(8,128)(2,1)}, u32[]{:S(2)}) copy-start(bf16[12,64,512]{2,1,0:T(8,128)(2,1)} %copy-done.17) | copy-start | bytes 2359300
  466.2 48.0 %copy-start.6 = (bf16[12,64,512]{2,1,0:T(8,128)(2,1)S(1)}, bf16[12,64,512]{2,1,0:T(8,128)(2,1)}, u32[]{:S(2)}) copy-start(bf16[12,64,512]{2,1,0:T(8,128)(2,1)} %copy-done.5) | copy-start | bytes 2359300
  506.7 7.5 copy-start.23
  511.9 3.1 copy-start.16
  511.9 3.1 copy-start.19
Sparse Core Ops, SparseCore 0:
  11.0 54.1 all-gather.6
  68.2 53.3 all-gather.8
  124.6 53.0 all-gather.10
  180.5 53.0 all-gather.12
  236.5 62.4 all-gather.14
  301.9 62.4 all-gather.16
  421.5 98.4 reduce-scatter.18
  526.7 97.9 reduce-scatter.20
  630.5 98.0 reduce-scatter.22
  735.2 97.9 reduce-scatter.12
  839.7 134.4 reduce-scatter.14
  981.6 134.5 reduce-scatter.16
where the time goes:
time: 1140 us; the launch traced here: 1120 us
  waiting for transfers between devices  859 us (75%)
  matrix products  115 us (10%)
  blocking collectives  80 us (7%)
  local copies, waits for them, and re-layouts  38.6 us (3%)
  other arithmetic  15.6 us (1%)
  between operations  15 us (1%)
    unnamed x15, waiting for transfers between devices  215 us
    reduce_scatter x1, waiting for transfers between devices, per_device(): lax.psum_scatter(outer_mat_grad, ('dp', 'fsdp'), scatter_dimension=0, til...  142 us
    reduce_scatter x1, waiting for transfers between devices, per_device(): lax.psum_scatter(inner_mat_grad, ('dp', 'fsdp'), scatter_dimension=0, til...  141 us
    reduce_scatter x1, waiting for transfers between devices, per_device(): lax.psum_scatter(output_mat_grad, ('dp', 'fsdp'), scatter_dimension=0, ti...  105 us
    unnamed x2, blocking collectives  80 us
    all_gather x1, waiting for transfers between devices, per_device(): lax.all_gather(inner_weight, ('dp', 'fsdp'), axis=0, tiled=True)  61.4 us
    all_gather x1, waiting for transfers between devices, per_device(): lax.all_gather(query_weight, ('dp', 'fsdp'), axis=0, tiled=True)  54 us
    all_gather x1, waiting for transfers between devices, per_device(): lax.all_gather(key_weight, ('dp', 'fsdp'), axis=0, tiled=True)  51.2 us
  transfers between devices with their start and end apart: 12, of which 12 were waited for; matrix products, arithmetic and copies ran while one was open for 9% of the time, Pallas kernels for 0%

commit v1 on v0

--- a/solution.py
+++ b/solution.py
@@ -70,7 +70,7 @@
     head_size = model_width // HEADS
     score_scale = head_size ** (-0.5)
     places = jnp.arange(frame_count, dtype=jnp.int32)
-    bounds = jnp.cumsum(lengths[0])
+    bounds = jnp.stack([lengths[0, 0], lengths[0, 0] + lengths[0, 1]])
     groups = jnp.sum((places[:, None] >= bounds[None, :]).astype(jnp.int32), axis=1)
     live_mask = (places < bounds[-1]).astype(jnp.float32)
     gathered = (
@@ -143,15 +143,6 @@
         second_offset.astype(jnp.float32),
     )
     layer_out = (normed_out * live_mask[:, None]).astype(jnp.bfloat16)
-    regathered = (
-        lax.all_gather(query_weight, ("dp", "fsdp"), axis=0, tiled=True),
-        lax.all_gather(key_weight, ("dp", "fsdp"), axis=0, tiled=True),
-        lax.all_gather(value_weight, ("dp", "fsdp"), axis=0, tiled=True),
-        lax.all_gather(output_weight, ("dp", "fsdp"), axis=0, tiled=True),
-        lax.all_gather(inner_weight, ("dp", "fsdp"), axis=0, tiled=True),
-        lax.all_gather(outer_weight, ("dp", "fsdp"), axis=0, tiled=True),
-    )
-    query_mat, key_mat, value_mat, output_mat, inner_mat, outer_mat = regathered
     grad_top = grad_out.astype(jnp.float32) * live_mask[:, None]
     grad_two, second_gain_grad, second_shift_grad = second_pull(grad_top)
     grad_outer = grad_two.astype(jnp.bfloat16)

time: 1140 us -> 1140 us (level)
  no operation moved by 1% of the time
where the time goes in v1:
time: 1140 us; the launch traced here: 1120 us
  waiting for transfers between devices  858 us (75%)
  matrix products  115 us (10%)
  blocking collectives  80 us (7%)
  local copies, waits for them, and re-layouts  39.3 us (3%)
  between operations  16.3 us (1%)
  other arithmetic  14.8 us (1%)
    unnamed x15, waiting for transfers between devices  215 us
    reduce_scatter x1, waiting for transfers between devices, per_device(): lax.psum_scatter(outer_mat_grad, ('dp', 'fsdp'), scatter_dimension=0, til...  142 us
    reduce_scatter x1, waiting for transfers between devices, per_device(): lax.psum_scatter(inner_mat_grad, ('dp', 'fsdp'), scatter_dimension=0, til...  141 us
    reduce_scatter x1, waiting for transfers between devices, per_device(): lax.psum_scatter(output_mat_grad, ('dp', 'fsdp'), scatter_dimension=0, ti...  105 us
    unnamed x2, blocking collectives  80 us
    all_gather x1, waiting for transfers between devices, per_device(): lax.all_gather(inner_weight, ('dp', 'fsdp'), axis=0, tiled=True)  61.4 us
    all_gather x1, waiting for transfers between devices, per_device(): lax.all_gather(query_weight, ('dp', 'fsdp'), axis=0, tiled=True)  54 us
    all_gather x1, waiting for transfers between devices, per_device(): lax.all_gather(key_weight, ('dp', 'fsdp'), axis=0, tiled=True)  51.2 us
  transfers between devices with their start and end apart: 12, of which 12 were waited for; matrix products, arithmetic and copies ran while one was open for 9% of the time, Pallas kernels for 0%

profile of v1, /device:TPU:24, one launch (start us, length us, event | category | flops | bytes accessed | tf_op | source)
XLA Modules:
  0.0 1123.4 jit_solution(13629870146439847360)
XLA Ops:
  11.2 0.8 dynamic-update-slice
  12.1 0.8 dynamic-update-slice.1
  12.9 0.8 dynamic-update-slice.2
  13.7 0.8 dynamic-update-slice.4
  14.6 0.8 dynamic-update-slice.3
  15.4 0.8 dynamic-update-slice.6
  16.2 0.8 dynamic-update-slice.8
  17.1 0.8 dynamic-update-slice.7
  17.9 0.8 dynamic-update-slice.5
  18.8 39.7 %all-reduce.19 = (bf16[768]{0:T(1024)(128)(2,1)S(1)}, bf16[768]{0:T(1024)(128)(2,1)S(1)}, bf16[768]{0:T(1024)(128)(2,1)S(1)}, bf16[768]{0:T(1024)(128)(2,1)S(1)}...) all-reduce(bf16[768]{0:T(1024)(128)(2,1)S(1)} %dynamic-update-slice, ...), channel_id=1, replica_groups=mesh['dp'=4,'fsdp'=8] {'dp','fsdp'}, use_global_device_ids=true, to_apply=%add | all-reduce | flops 9216 | bytes 36864
  58.5 1.3 fusion.35
  62.2 3.0 all-gather.7.cloned.1.call-done
  65.3 2.3 add_convert_fusion.3
  67.6 54.0 %all-gather.9.cloned.1.call-done = bf16[768,768]{1,0:T(8,128)(2,1)} async-done(((bf16[24,768]{1,0:T(8,128)(2,1)}), bf16[768,768]{1,0:T(8,128)(2,1)}) %all-gather.9.cloned.1.call-update) | async-done | bytes 1179664 | tf_op jit(solution)/shard_map/all_gather | solution.py:77
  121.6 2.9 add_convert_fusion.2
  124.8 1.7 copy.73
  126.5 51.2 %all-gather.11.cloned.1.call-done = bf16[768,768]{1,0:T(8,128)(2,1)} async-done(((bf16[24,768]{1,0:T(8,128)(2,1)}), bf16[768,768]{1,0:T(8,128)(2,1)}) %all-gather.11.cloned.1.call-update) | async-done | bytes 1179664 | tf_op jit(solution)/shard_map/all_gather | solution.py:79
  177.7 2.9 convolution_convert_fusion.1
  180.6 1.4 copy.74
  182.0 2.1 fusion.12
  184.1 2.6 fusion
  186.7 2.0 copy-done
  188.7 4.4 fusion.18
  193.0 40.6 %all-gather.13.cloned.1.call-done = bf16[768,768]{1,0:T(8,128)(2,1)} async-done(((bf16[24,768]{1,0:T(8,128)(2,1)}), bf16[768,768]{1,0:T(8,128)(2,1)}) %all-gather.13.cloned.1.call-update) | async-done | bytes 1179664 | tf_op jit(solution)/shard_map/all_gather | solution.py:82
  233.7 2.4 fusion.36
  236.1 1.1 copy-done.7
  237.6 61.4 %all-gather.15.cloned.1.call-done = bf16[768,3072]{1,0:T(8,128)(2,1)} async-done(((bf16[24,3072]{1,0:T(8,128)(2,1)}), bf16[768,3072]{1,0:T(8,128)(2,1)}) %all-gather.15.cloned.1.call-update) | async-done | bytes 4718608 | tf_op jit(solution)/shard_map/all_gather | solution.py:86
  299.0 21.0 %multiply_convert_fusion.1 = (bf16[512,3072]{1,0:T(8,128)(2,1)}, f32[512,3072]{1,0:T(8,128)}, f32[512,3072]{1,0:T(8,128)}) fusion(f32[3072]{0:T(1024)S(1)} %convert_element_type.159, bf16[768,3072]{1,0:T(8,128)(2,1)} %all-gather.15.cloned.1.call-done, f32[512,768]{1,0:T(8,128)} %copy-done.7, f32[768]{0:T(1024)S(1)} %convert_element_type.157, ...), kind=kOutput, calls=%fused_computation.14 | convolution fusion | flops 2521694208 | bytes 22042624 | tf_op jit(solution)/shard_map/dot_general | solution.py:20
  320.0 44.4 %all-gather.17.cloned.1.call-done = bf16[3072,768]{1,0:T(8,128)(2,1)} async-done(((bf16[96,768]{1,0:T(8,128)(2,1)}), bf16[3072,768]{1,0:T(8,128)(2,1)}) %all-gather.17.cloned.1.call-update) | async-done | bytes 4718608 | tf_op jit(solution)/shard_map/all_gather | solution.py:88
  364.4 6.1 fusion.37
  371.7 1.7 fusion.33
  374.3 8.7 convert_reduce_fusion
  383.0 3.1 multiply_reduce_fusion.2
  387.1 0.9 copy-done.14
  387.9 1.7 convolution_convert_fusion
  389.6 2.3 copy.76
  392.0 13.5 %multiply_reduce_fusion = (f32[12,512]{1,0:T(8,128)S(1)}, f32[12,512,512]{1,2,0:T(8,128)}) fusion(f32[12,512]{1,0:T(8,128)S(1)} %log_add_fusion, f32[12,512,512]{1,2,0:T(8,128)} %copy-done, pred[512,512]{0,1:T(8,128)(4,1)S(1)} %broadcast_compare_fusion, bf16[512,12,64]{0,2,1:T(8,128)(2,1)} %bitcast.82, bf16[512,12,64]{0,2,1:T(8,128)(2,1)} %bitcast.81), kind=kOutput, calls=%fused_computation.1 | convolution fusion | flops 418375680 | bytes 27049984 | tf_op jit(solution)/shard_map/qhd,khd->hqk/dot_general | solution.py:165
  405.5 7.0 multiply_convert_fusion
  412.5 1.2 convert_reduce_fusion.4
  413.7 1.4 copy-done.1
  415.1 0.9 copy-done.5
  416.0 2.2 convolution_bitcast_fusion.2
  418.3 3.1 copy.87
  421.6 4.8 multiply_convert_fusion.2
  426.4 0.9 copy-done.17
  427.3 2.2 convolution_bitcast_fusion.1
  429.5 3.2 copy.89
  432.8 6.6 convert_reduce_fusion.3
  439.4 0.9 copy-done.15
  440.3 2.2 convolution_bitcast_fusion
  442.5 3.1 copy.91
  445.8 3.7 fusion.40
  449.5 7.3 fusion.28
  456.9 1.1 copy-done.21
  458.0 8.2 fusion.41
  466.4 40.3 %all-reduce.18 = (f32[768]{0:T(1024)S(1)}, f32[768]{0:T(1024)S(1)}, f32[768]{0:T(1024)S(1)}, f32[768]{0:T(1024)S(1)}, f32[768]{0:T(1024)S(1)}, /*index=5*/f32[30...) all-reduce(f32[768]{0:T(1024)S(1)} %reduce_sum.228, ...), channel_id=3, replica_groups=mesh['dp'=4,'fsdp'=8] {'dp','fsdp'}, use_global_device_ids=true, to_apply=%region_14.15.clone | all-reduce | flops 9216 | bytes 73728
  511.9 2.2 fusion.39
  515.0 2.0 add_convert_fusion.1
  517.0 2.9 reduce-scatter.19.cloned.1.call-done
  519.9 104.8 %reduce-scatter.21.cloned.1.call-done = f32[24,768]{1,0:T(8,128)} async-done(((f32[768,768]{1,0:T(8,128)}), f32[24,768]{1,0:T(8,128)}) %reduce-scatter.21.cloned.1.call-update) | async-done | bytes 73744
  624.7 104.0 %reduce-scatter.23.cloned.1.call-done = f32[24,768]{1,0:T(8,128)} async-done(((f32[768,768]{1,0:T(8,128)}), f32[24,768]{1,0:T(8,128)}) %reduce-scatter.23.cloned.1.call-update) | async-done | bytes 73744
  728.7 104.6 %reduce-scatter.13.cloned.1.call-done = f32[24,768]{1,0:T(8,128)} async-done(((f32[768,768]{1,0:T(8,128)}), f32[24,768]{1,0:T(8,128)}) %reduce-scatter.13.cloned.1.call-update) | async-done | bytes 73744 | tf_op jit(solution)/shard_map/reduce_scatter | solution.py:204
  833.3 141.1 %reduce-scatter.15.cloned.1.call-done = f32[24,3072]{1,0:T(8,128)} async-done(((f32[768,3072]{1,0:T(8,128)}), f32[24,3072]{1,0:T(8,128)}) %reduce-scatter.15.cloned.1.call-update) | async-done | bytes 294928 | tf_op jit(solution)/shard_map/reduce_scatter | solution.py:208
  974.4 142.0 %reduce-scatter.17.cloned.1.call-done = f32[96,768]{1,0:T(8,128)} async-done(((f32[3072,768]{1,0:T(8,128)}), f32[96,768]{1,0:T(8,128)}) %reduce-scatter.17.cloned.1.call-update) | async-done | bytes 294928 | tf_op jit(solution)/shard_map/reduce_scatter | solution.py:210
  (130 shorter events, 15.3 us)
Async XLA Ops:
  7.2 114.4 %copy-start.2 = (bf16[512,768]{1,0:T(8,128)(2,1)S(1)}, bf16[512,768]{1,0:T(8,128)(2,1)}, u32[]{:S(2)}) copy-start(bf16[512,768]{1,0:T(8,128)(2,1)} %param.18) | copy-start | bytes 2359300
  7.2 58.1 %all-gather.7.cloned.1.call-start = ((), (), s32[]{:S(2)}) async-start(), calls=%async_computation.6 | async-start | bytes 1216512 | tf_op jit(solution)/shard_map/all_gather | solution.py:80
  7.9 113.7 %all-gather.9.cloned.1.call-start = ((), (), s32[]{:S(2)}) async-start(), calls=%async_computation.7 | async-start | bytes 1216512 | tf_op jit(solution)/shard_map/all_gather | solution.py:77
  8.7 169.0 %all-gather.11.cloned.1.call-start = ((), (), s32[]{:S(2)}) async-start(), calls=%async_computation.8 | async-start | bytes 1216512 | tf_op jit(solution)/shard_map/all_gather | solution.py:79
  9.4 224.3 %all-gather.13.cloned.1.call-start = ((), (), s32[]{:S(2)}) async-start(), calls=%async_computation.9 | async-start | bytes 1216512 | tf_op jit(solution)/shard_map/all_gather | solution.py:82
  10.0 289.0 %all-gather.15.cloned.1.call-start = ((), (), s32[]{:S(2)}) async-start(), calls=%async_computation.10 | async-start | bytes 4866048 | tf_op jit(solution)/shard_map/all_gather | solution.py:86
  10.6 353.8 %all-gather.17.cloned.1.call-start = ((), (), s32[]{:S(2)}) async-start(), calls=%async_computation.11 | async-start | bytes 4866048 | tf_op jit(solution)/shard_map/all_gather | solution.py:88
  11.2 508.8 %reduce-scatter.19.cloned.1.call-start = ((), (), s32[]{:S(2)}) async-start(), calls=%async_computation.15 | async-start | bytes 2433024
  124.8 61.9 %copy-start.11 = (bf16[512,768]{0,1:T(8,128)(2,1)}, bf16[512,768]{0,1:T(8,128)(2,1)S(1)}, u32[]{:S(2)}) copy-start(bf16[512,768]{0,1:T(8,128)(2,1)S(1)} %copy.72) | copy-start | bytes 2359300
  184.1 4.6 copy-start
  236.1 1.2 copy-start.7
  237.6 126.8 %copy-start.8 = (f32[512,768]{1,0:T(8,128)S(1)}, f32[512,768]{1,0:T(8,128)}, u32[]{:S(2)}) copy-start(f32[512,768]{1,0:T(8,128)} %copy-done.7) | copy-start | bytes 4718596
  364.4 6.4 copy-start.13
  371.6 2.6 copy-start.22
  373.4 9.6 slice-start.3
  373.6 9.3 copy-start.20
  374.3 8.7 slice-start.4
  382.9 3.2 copy-start.25
  383.0 3.2 copy-start.9
  386.2 1.8 copy-start.24
  387.0 0.9 copy-start.14
  392.0 13.5 %slice-start = ((s8[12582912]{0:T(1024)(128)(4,1)}), s8[4194304]{0:T(1024)(128)(4,1)S(1)}, s32[]{:S(2)}) async-start(s8[12582912]{0:T(1024)(128)(4,1)} %bitcast.72), calls=%async_computation.18 | async-start | bytes 8388608
  392.0 13.5 %slice-start.1 = ((s8[12582912]{0:T(1024)(128)(4,1)}), s8[4194304]{0:T(1024)(128)(4,1)S(1)}, s32[]{:S(2)}) async-start(s8[12582912]{0:T(1024)(128)(4,1)} %bitcast.72), calls=%async_computation.19 | async-start | bytes 8388608
  392.0 13.5 %slice-start.2 = ((s8[12582912]{0:T(1024)(128)(4,1)}), s8[4194304]{0:T(1024)(128)(4,1)S(1)}, s32[]{:S(2)}) async-start(s8[12582912]{0:T(1024)(128)(4,1)} %bitcast.72), calls=%async_computation.20 | async-start | bytes 8388608
  412.5 2.6 copy-start.1
  412.5 3.5 copy-start.3
  415.1 0.9 copy-start.5
  421.3 6.0 copy-start.4
  421.4 203.3 %reduce-scatter.21.cloned.1.call-start = ((), (), s32[]{:S(2)}) async-start(), calls=%async_computation.16 | async-start | bytes 2433024
  426.4 0.9 copy-start.17
  429.5 3.3 copy-start.12
  432.7 295.9 %reduce-scatter.23.cloned.1.call-start = ((), (), s32[]{:S(2)}) async-start(), calls=%async_computation.17 | async-start | bytes 2433024
  439.4 0.9 copy-start.15
  445.7 3.8 copy-start.10
  445.7 387.5 %reduce-scatter.13.cloned.1.call-start = ((), (), s32[]{:S(2)}) async-start(), calls=%async_computation.12 | async-start | bytes 2433024 | tf_op jit(solution)/shard_map/reduce_scatter | solution.py:204
  449.5 524.9 %reduce-scatter.15.cloned.1.call-start = ((), (), s32[]{:S(2)}) async-start(), calls=%async_computation.13 | async-start | bytes 9732096 | tf_op jit(solution)/shard_map/reduce_scatter | solution.py:208
  456.8 1.1 copy-start.21
  456.8 659.5 %reduce-scatter.17.cloned.1.call-start = ((), (), s32[]{:S(2)}) async-start(), calls=%async_computation.14 | async-start | bytes 9732096 | tf_op jit(solution)/shard_map/reduce_scatter | solution.py:210
  466.2 45.7 %copy-start.18 = (bf16[12,64,512]{2,1,0:T(8,128)(2,1)S(1)}, bf16[12,64,512]{2,1,0:T(8,128)(2,1)}, u32[]{:S(2)}) copy-start(bf16[12,64,512]{2,1,0:T(8,128)(2,1)} %copy-done.17) | copy-start | bytes 2359300
  466.2 48.0 %copy-start.6 = (bf16[12,64,512]{2,1,0:T(8,128)(2,1)S(1)}, bf16[12,64,512]{2,1,0:T(8,128)(2,1)}, u32[]{:S(2)}) copy-start(bf16[12,64,512]{2,1,0:T(8,128)(2,1)} %copy-done.5) | copy-start | bytes 2359300
  506.6 7.5 copy-start.23
  511.9 3.1 copy-start.16
  511.9 3.1 copy-start.19
Sparse Core Ops, SparseCore 0:
  11.0 54.1 all-gather.6
  68.2 53.3 all-gather.8
  124.6 53.0 all-gather.10
  180.5 53.0 all-gather.12
  236.5 62.4 all-gather.14
  301.9 62.4 all-gather.16
  421.5 98.4 reduce-scatter.18
  526.6 97.9 reduce-scatter.20
  630.6 98.0 reduce-scatter.22
  735.2 97.9 reduce-scatter.12
  839.7 134.5 reduce-scatter.14
  981.7 134.5 reduce-scatter.16

commit v2 on v1

--- a/solution.py
+++ b/solution.py
@@ -1,6 +1,11 @@
+import functools
+from types import SimpleNamespace
+
 import jax
 import jax.numpy as jnp
 from jax import lax
+from jax.experimental import pallas as pl
+from jax.experimental.pallas import tpu as pltpu
 from jax.sharding import PartitionSpec as P
 
 HEADS = 12
@@ -45,7 +50,7 @@
     return jnp.where(allowed[None], raw_scores, -1e30)
 
 
-def per_device(
+def general_device(
     frames,
     lengths,
     query_weight,
@@ -233,46 +238,939 @@
     )
 
 
+MESH = pl.DeviceIdType.MESH
+NZ = 4
+LANES = 128
+
+
+class Net:
+    def __init__(self):
+        dp, fs = lax.axis_index("dp"), lax.axis_index("fsdp")
+        self.y, self.c = lax.div(dp, 2), lax.rem(dp, 2)
+        self.z, self.x = lax.div(fs, 2), lax.rem(fs, 2)
+
+    def dev(self, y=None, c=None, z=None, x=None):
+        y = self.y if y is None else y
+        c = self.c if c is None else c
+        z = self.z if z is None else z
+        x = self.x if x is None else x
+        return (y * 2 + c, z * 2 + x)
+
+    def across(self, dim):
+        if dim == "x":
+            return self.dev(x=1 - self.x)
+        if dim == "y":
+            return self.dev(y=1 - self.y)
+        return self.dev(c=1 - self.c)
+
+    def barrier(self):
+        bar = pltpu.get_barrier_semaphore()
+
+        def tell(device):
+            pl.semaphore_signal(bar, inc=1, device_id=device, device_id_type=MESH)
+
+        for dim in "xyc":
+            tell(self.across(dim))
+        for k in range(1, NZ):
+            tell(self.dev(z=lax.rem(self.z + k, NZ)))
+        pl.semaphore_wait(bar, 3 + NZ - 1)
+
+
+class Way:
+    def __init__(self, net, region, order, sems, unit):
+        self.net, self.region, self.order = net, region, order
+        self.send, self.recv, self.unit = sems[0], sems[1], unit
+
+    def copy(self, src, dst, slot, device):
+        return pltpu.make_async_remote_copy(
+            src_ref=src, dst_ref=dst, send_sem=self.send.at[self.unit, slot],
+            recv_sem=self.recv.at[self.unit, slot], device_id=device, device_id_type=MESH)
+
+    def part(self, have="", **at):
+        n = self.net
+        for d in "yzx":
+            at.setdefault(d, None if d in have else getattr(n, d))
+        return self.region(at["y"], n.c, at["z"], at["x"])
+
+    def flip(self, *dims):
+        return {d: 1 - getattr(self.net, d) for d in dims}
+
+    def behind(self, k):
+        return lax.rem(self.net.z + NZ - k, NZ)
+
+    def ahead(self, k):
+        return lax.rem(self.net.z + k, NZ)
+
+
+class Gather(Way):
+    def along(self, k, have):
+        part = self.part(have)
+        return self.copy(part, part, k - 1, self.net.dev(z=self.ahead(k)))
+
+    def came(self, k, have):
+        part = self.part(have, z=self.behind(k))
+        return self.copy(part, part, k - 1, self.net.dev(z=self.behind(k)))
+
+    def over(self, slot, d, have, **at):
+        part = self.part(have, **at)
+        return self.copy(part, part, slot, self.net.across(d))
+
+    def sibling(self):
+        part = self.region(None, self.net.c, None, None)
+        return self.copy(part, part, 6, self.net.across("c"))
+
+    def stages(self):
+        first, d2, d3 = self.order
+        zs = range(1, NZ)
+
+        def start_a():
+            for k in zs:
+                self.along(k, "").start()
+
+        def start_b():
+            for k in zs:
+                self.came(k, "").wait_recv()
+            self.over(3, d2, "z").start()
+            self.over(4, d3, "z").start()
+
+        def start_c():
+            self.over(3, d2, "z").wait_recv()
+            self.over(5, d3, "z", **self.flip(d2)).start()
+
+        def start_d():
+            self.over(4, d3, "z").wait_recv()
+            self.over(5, d3, "z", **self.flip(d2)).wait_recv()
+            self.sibling().start()
+
+        def start_e():
+            self.sibling().wait_recv()
+
+        def end():
+            for k in zs:
+                self.along(k, "").wait_send()
+            self.over(3, d2, "z").wait_send()
+            self.over(4, d3, "z").wait_send()
+            self.over(5, d3, "z", **self.flip(d2)).wait_send()
+            self.sibling().wait_send()
+
+        if first == "z":
+            return dict(a=start_a, b=start_b, c=start_c, d=start_d, e=start_e, f=end)
+
+        have = first
+
+        def begin_a():
+            self.over(3, first, "").start()
+
+        def begin_b():
+            self.over(3, first, "").wait_recv()
+            for k in zs:
+                self.along(k, have).start()
+
+        def begin_c():
+            for k in zs:
+                self.came(k, have).wait_recv()
+            self.over(4, d3, have + "z").start()
+
+        def begin_d():
+            self.over(4, d3, have + "z").wait_recv()
+            self.sibling().start()
+
+        def finish():
+            self.over(3, first, "").wait_send()
+            for k in zs:
+                self.along(k, have).wait_send()
+            self.over(4, d3, have + "z").wait_send()
+            self.sibling().wait_send()
+
+        return dict(a=begin_a, b=begin_b, c=begin_c, d=begin_d, e=start_e, f=finish)
+
+
+class Scatter(Way):
+    def __init__(self, net, region, order, sems, unit, landing, line):
+        super().__init__(net, region, order, sems, unit)
+        self.landing, self.line = landing, line
+
+    def sibling(self, core):
+        part = self.region(None, core, None, None)
+        return self.copy(part, part, 6, self.net.across("c"))
+
+    def sibling_out(self):
+        return self.sibling(1 - self.net.c)
+
+    def sibling_in(self):
+        return self.sibling(self.net.c)
+
+    def over(self, k, d, slot, *dims):
+        return self.copy(self.part("z", **self.flip(*dims)), self.landing(k), slot, self.net.across(d))
+
+    def first(self):
+        return self.over(0, self.order[2], 4, self.order[2], self.order[1])
+
+    def second(self):
+        return self.over(1, self.order[2], 5, self.order[2])
+
+    def third(self):
+        return self.over(2, self.order[1], 3, self.order[1])
+
+    def along(self, k):
+        ahead = self.ahead(k)
+        return self.copy(self.part(z=ahead), self.line(k), k - 1, self.net.dev(z=ahead))
+
+    @staticmethod
+    def add(part, came):
+        part[...] = (part[...].astype(jnp.float32) + came[...].astype(jnp.float32)).astype(part.dtype)
+
+    def spread(self):
+        self.first().start()
+        self.second().start()
+
+    def fold_first(self):
+        self.first().wait_recv()
+        self.add(self.part("z", **self.flip(self.order[1])), self.landing(0))
+        self.third().start()
+
+    def fold_second(self):
+        self.second().wait_recv()
+        self.add(self.part("z"), self.landing(1))
+
+    def fold_third(self):
+        self.third().wait_recv()
+        self.add(self.part("z"), self.landing(2))
+        for k in range(1, NZ):
+            self.along(k).start()
+
+    def total(self):
+        out = self.part()[...].astype(jnp.float32)
+        for k in range(1, NZ):
+            self.along(k).wait_recv()
+            out = out + self.line(k)[...].astype(jnp.float32)
+        return out
+
+    def stages(self):
+        return dict(s=self.spread, t=self.fold_first, u=self.fold_second, v=self.fold_third)
+
+    def finish(self):
+        self.sibling_out().wait_send()
+        for one in (self.first(), self.second(), self.third()):
+            one.wait_send()
+        for k in range(1, NZ):
+            self.along(k).wait_send()
+
+
+def region_square(ref):
+    pair, half = ref.shape[2] // NZ, ref.shape[3] // 2
+
+    def region(y, c, z, x):
+        rows = pl.ds(0, pair * NZ) if z is None else pl.ds(pl.multiple_of(z * pair, 16), pair)
+        cols = pl.ds(0, half * 2) if x is None else pl.ds(pl.multiple_of(x * half, LANES), half)
+        return ref.at[pl.ds(0, 2) if y is None else y, c, rows, cols]
+
+    return region
+
+
+def region_lead(ref, start, size):
+    run = ref.shape[4] // 2
+
+    def region(y, c, z, x):
+        rows = pl.ds(0, 2 * run) if x is None else pl.ds(pl.multiple_of(x * run, 16), run)
+        high, low = (pl.ds(0, 2), pl.ds(0, 2)) if z is None else (lax.div(z, 2), lax.rem(z, 2))
+        return ref.at[pl.ds(0, 2) if y is None else y, c, high, low, rows, pl.ds(start, size)]
+
+    return region
+
+
+def region_small(ref):
+    def region(y, c, z, x):
+        return ref.at[pl.ds(0, 2) if y is None else y, c, pl.ds(0, NZ) if z is None else z, pl.ds(0, 2) if x is None else x]
+
+    return region
+
+
+UNITS = range(13)
+GATHER = ("zxy", "zyx", "zxy", "zyx", "zxy", "zyx", "zxy", "zyx", "zxy", "zyx", "zxy", "zyx", "zxy")
+SCATTER = ("zxy", "zyx", "zxy", "zyx", "zxy", "zyx", "zxy", "zyx", "zxy", "zyx", "zxy", "zyx", "zxy")
+OUTER = ((0, 256), (256, 256), (512, 128), (640, 128))
+
+
+def mm(left, right):
+    return jnp.dot(left, right, preferred_element_type=jnp.float32)
+
+
+def mm_nt(left, right):
+    return lax.dot_general(left, right, (((1,), (1,)), ((), ())), preferred_element_type=jnp.float32)
+
+
+def mm_tn(left, right):
+    return lax.dot_general(left, right, (((0,), (0,)), ((), ())), preferred_element_type=jnp.float32)
+
+
+def eights(block):
+    return jnp.sum(block.reshape(block.shape[0] // 8, 8, block.shape[1]), axis=0)
+
+
+STEP = 64
+F32, BF16 = jnp.float32, jnp.bfloat16
+
+
+def layer_kernel(names, *refs):
+    r = SimpleNamespace(**dict(zip(names, refs, strict=True)))
+    net = Net()
+    frame_count, width = r.frames.shape
+    half = width // 2
+    lead = r.wq.shape[0]
+    pair = 2 * lead
+    own_rows = pl.ds(pl.multiple_of(net.z * pair, 16), pair)
+    own_cols = pl.ds(pl.multiple_of(net.x * half, LANES), half)
+    w8, w2 = r.w8, r.w2
+    g2 = r.g2
+
+    x_in = pltpu.make_async_copy(r.frames, r.xbuf, r.isem.at[0])
+    g_in = pltpu.make_async_copy(r.grad_out, r.gbuf, r.isem.at[1])
+    x_in.start()
+    g_in.start()
+    net.barrier()
+
+    gather, scatter = [], []
+    for i in UNITS:
+        cols = OUTER[i - 8] if 8 <= i < 12 else None
+        if i < 8:
+            region = region_square(w8.at[i])
+            to = region_square(w2.at[i // 2, i % 2]) if i < 3 else region
+            landing = lambda k, i=i: r.land8.at[i, k]
+            line = lambda k, i=i: r.line8.at[i, k - 1]
+        elif cols:
+            region, to = region_lead(w2, *cols), region_lead(g2, *cols)
+            landing = lambda k, cols=cols: r.land2.at[k, :, :, :, pl.ds(*cols)]
+            line = lambda k, cols=cols: r.line2.at[k - 1, :, pl.ds(*cols)]
+        else:
+            region = region_small(r.small)
+        gather.append(Gather(net, region, GATHER[i], (r.gs, r.gr), i).stages())
+        if i < 12:
+            scatter.append(Scatter(net, to, SCATTER[i], (r.ss, r.sr), i, landing, line))
+
+    def shard(u):
+        if u < 4:
+            return (r.wq, r.wk, r.wv, r.wo)[u][...]
+        return r.wi[:, (u - 4) * width:(u - 3) * width]
+
+    def swap(u):
+        return pltpu.make_async_remote_copy(
+            src_ref=r.xs.at[u], dst_ref=r.xr.at[u], send_sem=r.xss.at[u], recv_sem=r.xrs.at[u],
+            device_id=net.across("x"), device_id_type=MESH)
+
+    def offer(u):
+        v = shard(u).astype(F32)
+        theirs = jnp.where(net.x == 0, v[:, half:], v[:, :half])
+        r.xs[u] = jnp.concatenate([theirs, jnp.zeros((8, half), F32)], axis=0).astype(BF16)
+        swap(u).start()
+
+    def merge(u):
+        swap(u).wait_recv()
+        v = shard(u).astype(F32)
+        mine = jnp.where(net.x == 0, v[:, :half], v[:, half:])
+        came = r.xr[u].astype(F32)[:lead]
+        first, second = jnp.where(net.x == 0, mine, came), jnp.where(net.x == 0, came, mine)
+        w8[u, net.y, net.c, own_rows, own_cols] = jnp.concatenate([first, second], axis=0).astype(BF16)
+
+    def place():
+        for k in range(4):
+            offer(k)
+        pack = r.pack
+        pack[...] = jnp.zeros_like(pack)
+        for row, one in enumerate((r.bq, None, r.bv, r.bo, r.g1, r.s1, r.b2, r.gg2, r.s2, r.bi1)):
+            if one is not None:
+                size = one.shape[0]
+                pack[row:row + 1, :size] = one[...].astype(F32).reshape(1, size)
+        r.small[net.y, net.c, net.z, net.x] = pack[...].astype(BF16)
+        w2[net.y, net.c, lax.div(net.z, 2), lax.rem(net.z, 2), pl.ds(pl.multiple_of(net.x * 4 * lead, 16), 4 * lead), :] = (
+            r.wouter[...])
+        for k in range(4, 8):
+            offer(k)
+
+    l0 = r.lengths[0, 0]
+    l1 = l0 + r.lengths[0, 1]
+    vec, bi, gsm, cs = r.vec, r.bi, r.gsm, r.cs
+    fa, q3, e12 = r.fa, r.q3, r.e12
+    act, gp, act_t = r.act, r.gp, r.act_t
+
+    def loop(body, step=STEP, total=frame_count):
+        def one(i, carry):
+            body(pl.ds(pl.multiple_of(i * step, step), step))
+            return carry
+
+        lax.fori_loop(0, total // step, one, 0)
+
+    def groups(shape, dim, start=0):
+        place = lax.broadcasted_iota(jnp.int32, shape, dim) + start
+        return (place >= l0).astype(jnp.int32) + (place >= l1).astype(jnp.int32)
+
+    def masks():
+        shape = (frame_count, LANES)
+        lane = lax.broadcasted_iota(jnp.int32, shape, 1)
+        group = groups(shape, 0)
+        for e in range(2):
+            spare = lane - (1 - e) * (LANES // 2)
+            inside = (spare >= 0) & (spare < 3)
+            r.mq[e] = jnp.where(inside & (spare != group), -1e30, 0.0).astype(BF16)
+            r.mk[e] = jnp.where(inside & (spare == group), 1.0, 0.0).astype(BF16)
+
+    def vectors():
+        got = r.small[...].reshape(32 * 16, LANES)
+        lane = lax.broadcasted_iota(jnp.int32, (LANES, width), 0)
+        col = lax.broadcasted_iota(jnp.int32, (LANES, width), 1)
+        tile = jnp.where((lane < lead) & (lane == lax.rem(col, lead)), 1.0, 0.0).astype(BF16)
+        wide = mm(got, tile).reshape(32, 16, width)
+        owner = lax.broadcasted_iota(jnp.int32, wide.shape, 0)
+        place = lax.div(lax.broadcasted_iota(jnp.int32, wide.shape, 2), lead)
+        vec[...] = jnp.sum(jnp.where(owner == place, wide, 0.0), axis=0)
+        inner = got.astype(F32).reshape(32, 16, LANES)[:, 9, :].astype(BF16)
+        for c in range(4):
+            lane = lax.broadcasted_iota(jnp.int32, (LANES, width), 0)
+            col = lax.broadcasted_iota(jnp.int32, (LANES, width), 1) + c * width
+            tile = jnp.where((lane < 4 * lead) & (lane == lax.rem(col, 4 * lead)), 1.0, 0.0).astype(BF16)
+            wide = mm(inner, tile)
+            owner = lax.broadcasted_iota(jnp.int32, wide.shape, 0)
+            place = lax.div(lax.broadcasted_iota(jnp.int32, wide.shape, 1) + c * width, 4 * lead)
+            bi[c] = jnp.sum(jnp.where(owner == place, wide, 0.0), axis=0, keepdims=True)
+
+    def square(u):
+        return w8[u].reshape(width, width)
+
+    def project(u):
+        rows = mm(r.xbuf[...], square(u)) + vec[pl.ds(u, 1), :]
+        q3[u] = (rows * 0.125 if u == 0 else rows).astype(BF16)
+
+    def head_lanes(shape, e):
+        return lax.div(lax.broadcasted_iota(jnp.int32, shape, 1), LANES // 2) == e
+
+    ROWS = 256
+
+    def attend(p):
+        cols = pl.ds(pl.multiple_of(p * LANES, LANES), LANES)
+        sides = []
+        for e in range(2):
+            mine = head_lanes((frame_count, LANES), e)
+            keys = jnp.where(mine, q3[1, :, cols], r.mk[e])
+            vals = jnp.where(mine, q3[2, :, cols], jnp.ones((), BF16))
+            sides.append((keys, vals))
+        for i in range(frame_count // ROWS):
+            rows = pl.ds(i * ROWS, ROWS)
+            outs = []
+            for e in range(2):
+                keys, vals = sides[e]
+                mine = head_lanes((ROWS, LANES), e)
+                query = jnp.where(mine, q3[0, rows, cols], r.mq[e, rows, :])
+                scores = mm_nt(query, keys)
+                top = jnp.max(scores, axis=1, keepdims=True)
+                weights = jnp.exp(scores - top).astype(BF16)
+                e12[2 * p + e, rows, :] = weights
+                outs.append(mm(weights, vals))
+            low = head_lanes((ROWS, LANES), 0)
+            over = jnp.where(low, outs[0], outs[1])
+            under = pltpu.roll(jnp.where(low, outs[1], outs[0]), LANES // 2, 1)
+            inverse = 1.0 / under
+            r.linv[rows, cols] = inverse
+            r.ctx[rows, cols] = (over * inverse).astype(BF16)
+
+    def heads(body, first, last):
+        def one(i, carry):
+            body(i)
+            return carry
+
+        lax.fori_loop(first, last, one, 0)
+
+    def norm_one():
+        fa[...] = mm(r.ctx[...], square(3))
+        r.ctx_t[...] = jnp.transpose(r.ctx[...]).reshape(r.ctx_t.shape)
+
+        def body(rows):
+            v = r.xbuf[rows, :].astype(F32) + fa[rows, :] + vec[3:4, :]
+            center = v - jnp.mean(v, axis=1, keepdims=True)
+            scale = lax.rsqrt(jnp.mean(center * center, axis=1, keepdims=True) + 1e-05)
+            normed = center * scale
+            r.n1[rows, :] = normed
+            r.r1[rows, :] = jnp.broadcast_to(scale, (STEP, LANES))
+            r.low[rows, :] = (normed * vec[4:5, :] + vec[5:6, :]).astype(BF16)
+
+        loop(body)
+        r.hid_t[...] = jnp.transpose(r.low[...]).reshape(r.hid_t.shape)
+
+    def feed(c):
+        fa[...] = mm(r.low[...], square(4 + c))
+
+        def body(rows):
+            v = fa[rows, :] + bi[c]
+            phi = 0.5 + 0.5 * lax.erf(v * 0.7071067811865476)
+            bell = jnp.exp(v * v * -0.5) * 0.3989422804014327
+            act[c, rows, :] = (v * phi).astype(BF16)
+            gp[c, rows, :] = (phi + v * bell).astype(BF16)
+
+        loop(body, 32)
+        act_t[c // 2, c % 2] = jnp.transpose(act[c])
+
+    def block(ref, c):
+        return ref[c // 2, c % 2].reshape(width, width)
+
+    def feed_out(k):
+        start, size = OUTER[k]
+        cols = slice(start, start + size)
+        total = None
+        for c in range(4):
+            one = mm(act[c], w2[c // 2, c % 2, :, :, :, cols].reshape(width, size))
+            total = one if total is None else total + one
+        fa[:, cols] = total
+
+    def fold(slot, row):
+        gsm[row:row + 1, :] = jnp.sum(cs[slot], axis=0, keepdims=True)
+
+    def norm_two():
+        g_in.wait()
+        cs[...] = jnp.zeros_like(cs)
+
+        def body(rows):
+            hidden = r.n1[rows, :] * vec[4:5, :] + vec[5:6, :]
+            v = hidden + fa[rows, :] + vec[6:7, :]
+            center = v - jnp.mean(v, axis=1, keepdims=True)
+            scale = lax.rsqrt(jnp.mean(center * center, axis=1, keepdims=True) + 1e-05)
+            normed = center * scale
+            place = lax.broadcasted_iota(jnp.int32, normed.shape, 0) + rows.start
+            live = jnp.where(place < l1, 1.0, 0.0)
+            r.xbuf[rows, :] = ((normed * vec[7:8, :] + vec[8:9, :]) * live).astype(BF16)
+            top = r.gbuf[rows, :].astype(F32) * live
+            e = top * vec[7:8, :]
+            d = e - jnp.mean(e, axis=1, keepdims=True) - normed * jnp.mean(e * normed, axis=1, keepdims=True)
+            d = d * scale
+            r.d2[rows, :] = d
+            low = d.astype(BF16)
+            r.low[rows, :] = low
+            cs[0] += eights(top * normed)
+            cs[1] += eights(top)
+            cs[2] += eights(low.astype(F32))
+
+        loop(body)
+        fold(0, 7)
+        fold(1, 8)
+        fold(2, 6)
+
+    layer_out = pltpu.make_async_copy(r.xbuf, r.layer_out, r.isem.at[0])
+    frames_out = pltpu.make_async_copy(r.gbuf, r.frames_grad, r.isem.at[1])
+
+    def back_feed(c):
+        fa[...] = mm_nt(r.low[...], block(w2, c))
+        cs[0] = jnp.zeros_like(cs[0])
+
+        def body(rows):
+            low = (fa[rows, :] * gp[c, rows, :].astype(F32)).astype(BF16)
+            gp[c, rows, :] = low
+            cs[0] += eights(low.astype(F32))
+
+        loop(body)
+        fold(0, 9 + c)
+
+    def grad_square(u, left, right, own):
+        core = net.c if own else 1 - net.c
+        to = w2.at[u // 2, u % 2] if u < 3 else w8.at[u]
+        rows = mm(left[:, core].reshape(2 * pair * NZ, frame_count), right()).reshape(2, pair * NZ, width)
+        if own:
+            scatter[u].sibling_in().wait_recv()
+            rows = rows + to[:, core].astype(F32)
+        to[:, core] = rows.astype(BF16)
+
+    def grad_outer(i, own):
+        core = net.c if own else 1 - net.c
+        start, size = OUTER[i - 8]
+        cols = pl.ds(start, size)
+        left = act_t[:, core].reshape(2 * width, frame_count)
+        rows = mm(left, r.low[:, cols]).reshape((2,) + g2.shape[2:5] + (size,))
+        if own:
+            scatter[i].sibling_in().wait_recv()
+            rows = rows + g2[:, core, :, :, :, cols].astype(F32)
+        g2[:, core, :, :, :, cols] = rows.astype(BF16)
+
+    def back_hidden():
+        def one(c, carry):
+            got = mm_nt(gp[c], w8[4 + c].reshape(width, width))
+
+            @pl.when(c == 0)
+            def _():
+                fa[...] = got
+
+            @pl.when(c > 0)
+            def _():
+                fa[...] += got
+
+            return carry
+
+        lax.fori_loop(0, 4, one, 0)
+
+    def back_norm_one():
+        cs[...] = jnp.zeros_like(cs)
+
+        def body(rows):
+            d = r.d2[rows, :] + fa[rows, :]
+            normed = r.n1[rows, :]
+            e = d * vec[4:5, :]
+            cs[0] += eights(d * normed)
+            cs[1] += eights(d)
+            d = e - jnp.mean(e, axis=1, keepdims=True) - normed * jnp.mean(e * normed, axis=1, keepdims=True)
+            d = d * r.r1[rows, 0:1]
+            r.d2[rows, :] = d
+            low = d.astype(BF16)
+            r.low[rows, :] = low
+            cs[2] += eights(low.astype(F32))
+
+        loop(body)
+        fold(0, 4)
+        fold(1, 5)
+        fold(2, 3)
+
+    def back_context():
+        act[3] = mm_nt(r.low[...], square(3)).astype(BF16)
+
+    def back_attend(p):
+        cols = pl.ds(pl.multiple_of(p * LANES, LANES), LANES)
+        shape = (frame_count, LANES)
+        low = head_lanes(shape, 0)
+        scaled = (act[3, :, cols].astype(F32) * r.linv[:, cols]).astype(BF16)
+        product = scaled.astype(F32) * r.ctx[:, cols].astype(F32)
+        lane = lax.broadcasted_iota(jnp.int32, shape, 1)
+        k2, v2, q2 = q3[1, :, cols], q3[2, :, cols], q3[0, :, cols]
+        dq, dk, dv = [], [], []
+        for e in range(2):
+            mine = head_lanes(shape, e)
+            spare = lane - (1 - e) * (LANES // 2)
+            dot = jnp.sum(jnp.where(mine, product, 0.0), axis=1, keepdims=True)
+            high = dot.astype(BF16).astype(F32)
+            extra = jnp.where(spare == 0, high, jnp.where(spare == 1, dot - high, 0.0)).astype(BF16)
+            left = jnp.where(mine, scaled, extra)
+            minus = jnp.where((spare == 0) | (spare == 1), -1.0, 0.0).astype(BF16)
+            right = jnp.where(mine, v2, minus)
+            for i in range(frame_count // ROWS):
+                part = slice(i * ROWS, (i + 1) * ROWS)
+                r.ds[e, part, :] = (e12[2 * p + e, part, :].astype(F32) * mm_nt(left[part], right)).astype(BF16)
+            dq.append(mm(r.ds[e], k2))
+            dk.append(mm_tn(r.ds[e], q2))
+            dv.append(mm_tn(e12[2 * p + e], scaled))
+        act[0, :, cols] = (jnp.where(low, dq[0], dq[1]) * 0.125).astype(BF16)
+        act[1, :, cols] = jnp.where(low, dk[0], dk[1]).astype(BF16)
+        act[2, :, cols] = jnp.where(low, dv[0], dv[1]).astype(BF16)
+
+    def bias_sums():
+        cs[...] = jnp.zeros_like(cs)
+
+        def body(rows):
+            cs[0] += eights(act[0, rows, :].astype(F32))
+            cs[1] += eights(act[2, rows, :].astype(F32))
+
+        loop(body)
+        fold(0, 0)
+        fold(1, 2)
+        gsm[1:2, :] = jnp.zeros((1, width), F32)
+        gsm[13:16, :] = jnp.zeros((3, width), F32)
+
+    def back_frames():
+        fa[...] = r.d2[...] + mm_nt(act[0], square(0))
+        fa[...] += mm_nt(act[1], square(1))
+        layer_out.wait()
+        r.gbuf[...] = (fa[...] + mm_nt(act[2], square(2))).astype(BF16)
+        frames_out.start()
+
+    def small_copy(k, device):
+        return pltpu.make_async_remote_copy(
+            src_ref=r.sm.at[k], dst_ref=r.sl.at[k], send_sem=r.sms.at[k], recv_sem=r.smr.at[k],
+            device_id=device, device_id_type=MESH)
+
+    def small_step(k):
+        if k == 0:
+            r.sm[0] = gsm[...]
+        else:
+            r.sm[k] = r.sm[k - 1] + r.sl[k - 1]
+        if k < 3:
+            small_copy(k, net.across("cyx"[k])).start()
+
+    def small_wait(k):
+        small_copy(k, net.across("cyx"[k])).wait_recv()
+
+    def small_line(k):
+        return pltpu.make_async_remote_copy(
+            src_ref=r.sm.at[3], dst_ref=r.sl.at[2 + k], send_sem=r.sms.at[2 + k], recv_sem=r.smr.at[2 + k],
+            device_id=net.dev(z=lax.rem(net.z + k, NZ)), device_id_type=MESH)
+
+    def small_total():
+        for k in range(1, NZ):
+            small_line(k).wait_recv()
+        whole = r.sm[3] + r.sl[3] + r.sl[4] + r.sl[5]
+        index = (net.y * 2 + net.c) * 2 * NZ + net.z * 2 + net.x
+        turned = pltpu.roll(whole, lax.rem(width - index * lead, width), 1)
+        row = lax.broadcasted_iota(jnp.int32, (16, width), 0)
+        block = lax.div(index, 8)
+        inner = jnp.sum(jnp.where(row == 9 + block, whole, 0.0), axis=0, keepdims=True)
+        inner = pltpu.roll(jnp.broadcast_to(inner, (8, width)), lax.rem(width - lax.rem(index, 8) * 4 * lead, width), 1)
+        r.gsmall[0:8, :] = turned[0:8, :LANES]
+        r.gsmall[8:16, :] = jnp.where(row[:8, :LANES] == 0, turned[8:9, :LANES], inner[:, :LANES])
+
+    def swap_back(u):
+        return pltpu.make_async_remote_copy(
+            src_ref=r.ys.at[u], dst_ref=r.yr.at[u], send_sem=r.yss.at[u], recv_sem=r.yrs.at[u],
+            device_id=net.across("x"), device_id_type=MESH)
+
+    def out_of(u):
+        if u < 4:
+            return (r.gwq, r.gwk, r.gwv, r.gwo)[u], 0
+        return r.gwi, (u - 4) * width
+
+    def total_square(u):
+        r.f8[...] = scatter[u].total()
+        out, start = out_of(u)
+        mine, theirs = pl.multiple_of(net.x * lead, 8), pl.multiple_of((1 - net.x) * lead, 8)
+        r.ys[u] = r.f8[pl.ds(theirs, lead), :]
+        swap_back(u).start()
+        out[:, pl.ds(pl.multiple_of(start + net.x * half, LANES), half)] = r.f8[pl.ds(mine, lead), :]
+
+    def last_square(u):
+        swap_back(u).wait_recv()
+        out, start = out_of(u)
+        out[:, pl.ds(pl.multiple_of(start + (1 - net.x) * half, LANES), half)] = r.yr[u]
+
+    def total_outer(i):
+        r.gwouter[:, pl.ds(*OUTER[i - 8])] = scatter[i].total()
+
+    def unit(i, left=None, right=None):
+        steps = SimpleNamespace(**gather[i])
+        if i == len(UNITS) - 1:
+            return steps
+        way, square = scatter[i], i < 8
+
+        def half_of(own):
+            if square:
+                grad_square(i, left, right, own)
+            else:
+                grad_outer(i, own)
+
+        def away():
+            half_of(False)
+            way.sibling_out().start()
+
+        def home():
+            half_of(True)
+            way.spread()
+
+        steps.away, steps.home = away, home
+        steps.t, steps.u, steps.v = way.fold_first, way.fold_second, way.fold_third
+        if square:
+            steps.p = functools.partial(merge, i)
+            steps.x, steps.y = functools.partial(total_square, i), functools.partial(last_square, i)
+        else:
+            steps.x = functools.partial(total_outer, i)
+        return steps
+
+    def give(k):
+        pl.semaphore_signal(r.free.at[k], inc=1, device_id=net.across("c"), device_id_type=MESH)
+
+    def take(k):
+        pl.semaphore_wait(r.free.at[k], 1)
+
+    def turn():
+        x_in.wait()
+        r.xt[...] = jnp.transpose(r.xbuf[...]).reshape(r.xt.shape)
+
+    def gather_end():
+        for one in gather:
+            one["f"]()
+
+    def small(k):
+        if k > 0:
+            small_wait(k - 1)
+        small_step(k)
+        if k == 3:
+            for one in range(1, NZ):
+                small_line(one).start()
+
+    def end():
+        for one in scatter:
+            one.finish()
+        for u in range(8):
+            swap(u).wait_send()
+            swap_back(u).wait_send()
+        for k in range(3):
+            small_copy(k, net.across("cyx"[k])).wait_send()
+        for k in range(1, NZ):
+            small_line(k).wait_send()
+        frames_out.wait()
+
+    def go(*steps):
+        for step in steps:
+            step()
+
+    q, k, v = (unit(u, r.xt, lambda u=u: act[u]) for u in range(3))
+    o = unit(3, r.ctx_t, lambda: r.low[...])
+    i0, i1, i2, i3 = (unit(4 + u, r.hid_t, lambda u=u: gp[u]) for u in range(4))
+    w0, w1, w2_, w3 = (unit(8 + u) for u in range(4))
+    s = unit(12)
+    place()
+    go(s.a, q.p, k.p, q.a, k.a, v.p, o.p)
+    masks()
+    turn()
+    go(s.b, s.c, s.d, q.b, k.b, v.a, o.a, s.e)
+    vectors()
+    go(i0.p, i1.p, q.c, k.c, v.b, o.b, i0.a, i1.a, q.d, k.d, i2.p, i3.p)
+    go(v.c, o.c, i0.b, i1.b, i2.a, i3.a, q.e, k.e, v.d, o.d)
+    project(0)
+    project(1)
+    go(i0.c, i1.c, i2.b, i3.b, w0.a, w1.a, v.e, o.e, i0.d, i1.d)
+    project(2)
+    heads(attend, 0, 2)
+    go(i2.c, i3.c, w0.b, w1.b, w2_.a, w3.a, i0.e, i1.e, i2.d, i3.d)
+    heads(attend, 2, 4)
+    heads(attend, 4, 6)
+    norm_one()
+    go(w0.c, w1.c, w2_.b, w3.b, i2.e, i3.e, w0.d, w1.d)
+    feed(0)
+    feed(1)
+    go(w2_.c, w3.c, w0.e, w1.e)
+    feed(2)
+    feed(3)
+    feed_out(0)
+    feed_out(1)
+    go(w2_.d, w3.d, w2_.e)
+    feed_out(2)
+    go(w3.e)
+    feed_out(3)
+    norm_two()
+    layer_out.start()
+    go(w0.away, w1.away, w0.home, w1.home, w2_.away, w2_.home, w3.away, w3.home)
+    gather_end()
+    back_feed(0)
+    back_feed(1)
+    back_feed(2)
+    back_feed(3)
+    give(0)
+    go(w0.t, w1.t, w0.u, w1.u)
+    back_hidden()
+    give(1)
+    go(w2_.t, w3.t, w2_.u, w3.u)
+    take(1)
+    go(i0.away, i1.away, i0.home, i1.home, w0.v, w1.v, i2.away, i3.away, i2.home, i3.home)
+    back_norm_one()
+    back_context()
+    give(2)
+    go(w2_.v, w3.v)
+    take(2)
+    go(o.away, o.home, i0.t, i1.t, i0.u, i1.u, w0.x, w1.x, i2.t, i3.t, i2.u, i3.u)
+    heads(back_attend, 0, 2)
+    go(w2_.x, w3.x, o.t, i0.v, i1.v, o.u)
+    heads(back_attend, 2, 4)
+    go(i2.v, i3.v, i0.x, i1.x)
+    heads(back_attend, 4, 6)
+    take(0)
+    go(q.away, k.away, q.home, k.home, v.away, v.home)
+    bias_sums()
+    small(0)
+    go(i2.x, i3.x, o.v, q.t, k.t, v.t)
+    back_frames()
+    small(1)
+    go(q.u, k.u, v.u)
+    small(2)
+    go(o.x, q.v, k.v, v.v)
+    small(3)
+    go(q.x, k.x, v.x)
+    small_total()
+    go(i0.y, i1.y, i2.y, i3.y, o.y, q.y, k.y, v.y)
+    end()
+
+
+def kernel_device(
+    frames, lengths, query_weight, query_bias, key_weight, value_weight, value_bias, output_weight, output_bias,
+    first_gain, first_shift, inner_weight, inner_bias, outer_weight, outer_bias, second_gain, second_shift, grad_out,
+):
+    count, width = frames.shape
+    lead = query_weight.shape[0]
+    pair, half = 2 * lead, width // 2
+    vmem, hbm = pl.BlockSpec(memory_space=pltpu.VMEM), pl.BlockSpec(memory_space=pl.ANY)
+    smem = pl.BlockSpec(memory_space=pltpu.SMEM)
+    args = dict(
+        frames=(hbm, frames), grad_out=(hbm, grad_out), lengths=(smem, lengths), wq=(vmem, query_weight),
+        wk=(vmem, key_weight), wv=(vmem, value_weight), wo=(vmem, output_weight), wi=(vmem, inner_weight),
+        wouter=(vmem, outer_weight), bq=(vmem, query_bias), bv=(vmem, value_bias), bo=(vmem, output_bias),
+        g1=(vmem, first_gain), s1=(vmem, first_shift), b2=(vmem, outer_bias), gg2=(vmem, second_gain),
+        s2=(vmem, second_shift), bi1=(vmem, inner_bias))
+    shape = jax.ShapeDtypeStruct
+    outs = dict(
+        layer_out=(hbm, shape((count, width), BF16)), frames_grad=(hbm, shape((count, width), BF16)),
+        gwq=(vmem, shape((lead, width), F32)), gwk=(vmem, shape((lead, width), F32)),
+        gwv=(vmem, shape((lead, width), F32)), gwo=(vmem, shape((lead, width), F32)),
+        gwi=(vmem, shape(inner_weight.shape, F32)), gwouter=(vmem, shape(outer_weight.shape, F32)),
+        gsmall=(vmem, shape((16, LANES), F32)))
+    dma = pltpu.SemaphoreType.DMA
+    big = (count, width)
+    square = (2, 2, pair * NZ, width)
+    turned = (2, 2, pair * NZ, count)
+    lead_shape = (2, 2, 2, 2, 8 * lead, width)
+    scratch = dict(
+        w8=((8,) + square, BF16), w2=(lead_shape, BF16), g2=(lead_shape, BF16), small=((2, 2, NZ, 2, 16, LANES), BF16),
+        land8=((8, 3, pair * NZ, half), BF16), line8=((8, NZ - 1, pair, half), BF16),
+        land2=((3, 2, 2, 4 * lead, width), BF16), line2=((NZ - 1, 4 * lead, width), BF16),
+        pack=((16, LANES), F32), xs=((8, lead + 8, half), BF16), xr=((8, lead + 8, half), BF16),
+        ys=((8, lead, half), F32), yr=((8, lead, half), F32), xbuf=(big, BF16), gbuf=(big, BF16), q3=((3,) + big, BF16),
+        e12=((HEADS, count, count), BF16), linv=(big, F32), ctx=(big, BF16), xt=(turned, BF16), ctx_t=(turned, BF16),
+        hid_t=(turned, BF16), low=(big, BF16), n1=(big, F32), r1=((count, LANES), F32), act=((4,) + big, BF16),
+        gp=((4,) + big, BF16), act_t=((2, 2, width, count), BF16), fa=(big, F32), d2=(big, F32),
+        ds=((2, count, count), BF16), mq=((2, count, LANES), BF16), mk=((2, count, LANES), BF16), vec=((16, width), F32),
+        bi=((4, 1, width), F32), gsm=((16, width), F32), cs=((3, 8, width), F32), sm=((4, 16, width), F32),
+        sl=((6, 16, width), F32), f8=((pair, half), F32))
+    scratch = {k: pltpu.VMEM(*v) for k, v in scratch.items()}
+    scratch.update(
+        gs=dma((13, 7)), gr=dma((13, 7)), ss=dma((12, 7)), sr=dma((12, 7)), xss=dma((8,)), xrs=dma((8,)), yss=dma((8,)),
+        yrs=dma((8,)), sms=dma((6,)), smr=dma((6,)), isem=dma((2,)), free=pltpu.SemaphoreType.REGULAR((3,)))
+    got = pl.pallas_call(
+        functools.partial(layer_kernel, (*args, *outs, *scratch)),
+        out_shape=[o[1] for o in outs.values()],
+        in_specs=[a[0] for a in args.values()],
+        out_specs=[o[0] for o in outs.values()],
+        scratch_shapes=list(scratch.values()),
+        compiler_params=pltpu.CompilerParams(collective_id=0, has_side_effects=True, vmem_limit_bytes=VMEM_BYTES),
+    )(*(a[1] for a in args.values()))
+
+    bias, wide = shape((lead,), F32), shape((4 * lead,), F32)
+    vectors = {3: bias, 6: bias, 8: bias, 9: bias, 10: bias, 12: wide, 14: bias, 15: bias, 16: bias}
+    row_of = {3: 0, 6: 2, 8: 3, 9: 4, 10: 5, 12: 9, 14: 6, 15: 7, 16: 8}
+    places = [i for i in range(17) if i not in vectors]
+
+    def publish(*refs):
+        came, small, out = refs[:8], refs[8], refs[9:]
+        for a, i in zip(came, places, strict=True):
+            out[i][...] = a[...]
+        for i, row in row_of.items():
+            size = vectors[i].shape[0]
+            out[i][...] = small[row:row + 1, :size].reshape(size)
+
+    whole = dict(zip(places, (o[1] for o in list(outs.values())[:8]), strict=True))
+    return tuple(pl.pallas_call(
+        publish,
+        out_shape=[vectors[i] if i in vectors else whole[i] for i in range(17)],
+        in_specs=[vmem] * 9,
+        out_specs=[vmem] * 17,
+    )(*got))
+
+
+VMEM_BYTES = 63 << 20
+
+
 def solution(mesh):
+    split = P(("dp", "fsdp"))
+    rows = P(("dp", "fsdp"), None)
     in_specs = (
-        P(("dp", "fsdp"), None),
-        P(("dp", "fsdp"), None),
-        P(("dp", "fsdp"), None),
-        P(("dp", "fsdp")),
-        P(("dp", "fsdp"), None),
-        P(("dp", "fsdp"), None),
-        P(("dp", "fsdp")),
-        P(("dp", "fsdp"), None),
-        P(("dp", "fsdp")),
-        P(("dp", "fsdp")),
-        P(("dp", "fsdp")),
-        P(("dp", "fsdp"), None),
-        P(("dp", "fsdp")),
-        P(("dp", "fsdp"), None),
-        P(("dp", "fsdp")),
-        P(("dp", "fsdp")),
-        P(("dp", "fsdp")),
-        P(("dp", "fsdp"), None),
+        rows, rows, rows, split, rows, rows, split, rows, split, split, split, rows, split, rows, split, split, split, rows,
     )
     out_specs = (
-        P(("dp", "fsdp"), None),
-        P(("dp", "fsdp"), None),
-        P(("dp", "fsdp"), None),
-        P(("dp", "fsdp")),
-        P(("dp", "fsdp"), None),
-        P(("dp", "fsdp"), None),
-        P(("dp", "fsdp")),
-        P(("dp", "fsdp"), None),
-        P(("dp", "fsdp")),
-        P(("dp", "fsdp")),
-        P(("dp", "fsdp")),
-        P(("dp", "fsdp"), None),
-        P(("dp", "fsdp")),
-        P(("dp", "fsdp"), None),
-        P(("dp", "fsdp")),
-        P(("dp", "fsdp")),
-        P(("dp", "fsdp")),
-    )
-    return jax.shard_map(
-        per_device, mesh=mesh, in_specs=in_specs, out_specs=out_specs, check_vma=False
-    )
+        rows, rows, rows, split, rows, rows, split, rows, split, split, split, rows, split, rows, split, split, split,
+    )
+    fits = mesh.shape["dp"] == 4 and mesh.shape["fsdp"] == 2 * NZ
+
+    def per_device(frames, lengths, query_weight, *rest):
+        lead, width = query_weight.shape
+        good = fits and lead % 8 == 0 and 4 * lead <= LANES and width == 768
+        run = kernel_device if good else general_device
+        return run(frames, lengths, query_weight, *rest)
+
+    return jax.shard_map(per_device, mesh=mesh, in_specs=in_specs, out_specs=out_specs, check_vma=False)

time: 1140 us -> 200 us (0.18); the launches traced: 1120 us -> 196 us
  waiting for transfers between devices: 858 us -> 0 us
  Pallas kernels: 0 us -> 195 us
  matrix products: 115 us -> 0 us
  blocking collectives: 80 us -> 0 us
  local copies, waits for them, and re-layouts: 39.3 us -> 0 us
  between operations: 16.3 us -> 0.96 us
  other arithmetic: 14.8 us -> 0 us
    reduce_scatter x3 -> x0, waiting for transfers between devices: 388 us -> none  [the longest x1 142 us: per_device(): lax.psum_scatter(outer_mat_grad, ('dp', 'fsdp'), scatter_dimension=0, til...]
    all_gather x6 -> x0, waiting for transfers between devices: 255 us -> none  [the longest x1 61.4 us: per_device(): lax.all_gather(inner_weight, ('dp', 'fsdp'), axis=0, tiled=True)]
    unnamed x15 -> x0, waiting for transfers between devices: 215 us -> none
    pallas_call x0 -> x2, Pallas kernels: none -> 195 us  [the longest x1 192 us: kernel_device(): pl.pallas_call(functools.partial(layer_kernel, (*args, *outs, *scratch)),...]
    dot_general x24 -> x0, matrix products: 115 us -> none  [the longest x6 37.7 us: matmul(): return jnp.dot(left_side, right_side, preferred_element_type=jnp.float32)]
    unnamed x2 -> x0, blocking collectives: 80 us -> none
    unnamed x92 -> x0, local copies, waits for them, and re-layouts: 32.1 us -> none
  transfers between devices with their start and end apart: 12 -> 0, of which waited for: 12 -> 0; matrix products, arithmetic and copies ran while one was open for 9% -> 0% of each run, Pallas kernels for 0% -> 0%
where the time goes in v2:
time: 200 us; the launch traced here: 196 us
  Pallas kernels  195 us (98%)
    pallas_call x1, Pallas kernels, kernel_device(): pl.pallas_call(functools.partial(layer_kernel, (*args, *outs, *scratch)),...  192 us

profile of v2, /device:TPU:24, one launch (start us, length us, event | category | flops | bytes accessed | tf_op | source)
XLA Modules:
  0.0 196.3 jit_solution(2746431529621113577)
XLA Ops:
  0.7 192.2 %shard_map.305 = (bf16[512,768]{1,0:T(8,128)(2,1)}, bf16[512,768]{1,0:T(8,128)(2,1)}, f32[24,768]{1,0:T(8,128)}, f32[24,768]{1,0:T(8,128)}, f32[24,768]{1,0:T(8,...) custom-call(bf16[512,768]{1,0:T(8,128)(2,1)} %refs_0_.1, ...), custom_call_target="tpu_custom_call" | custom-call | tf_op jit(solution)/shard_map/pallas_call | solution.py:1125
  192.9 3.1 %shard_map.306 = (bf16[512,768]{1,0:T(8,128)(2,1)}, bf16[512,768]{1,0:T(8,128)(2,1)}, f32[24,768]{1,0:T(8,128)}, f32[24]{0:T(128)}, f32[24,768]{1,0:T(8,128)}, /...) custom-call(bf16[512,768]{1,0:T(8,128)(2,1)} %get-tuple-element.26.r, ...), custom_call_target="tpu_custom_call" | custom-call | tf_op jit(solution)/shard_map/pallas_call | solution.py:1148
